TPU v7x, 32 devices: a whole 2x2x4 slice. The times are simulated.
32 devices in a mesh: tm: 4 (over z), gx: 4 (over x, core), gy: 2 (over y).
Axes of the slice: x: 2, y: 2, z: 4, core: 2. Of those that a mesh axis runs over, the one named last changes fastest.
Arguments:
- lagrange: float32 [8, 8, 256, 256], P('tm', None, 'gx', 'gy'), may hold values from -6 to 6
- obs_lagrange: float32 [8, 4, 2, 1024], P('tm', 'gx', 'gy'), may hold values from -6 to 6
- increment: float32 [8, 8, 256, 256], P('tm', None, 'gx', 'gy'), may hold values from -6 to 6
- forcing: float32 [8, 8, 256, 256], P('tm', None, 'gx', 'gy'), may hold values from -6 to 6
- departures: float32 [8, 4, 2, 1024], P('tm', 'gx', 'gy'), may hold values from -6 to 6
- model_var: float32 [8, 8, 256, 256], P('tm', None, 'gx', 'gy'), may hold values from 0.3 to 3
- obs_var: float32 [8, 4, 2, 1024], P('tm', 'gx', 'gy'), may hold values from 0.5 to 2
- wind_east: float32 [8, 8, 256, 256], P('tm', None, 'gx', 'gy'), may hold values from -0.3 to 0.3
- wind_north: float32 [8, 8, 256, 256], P('tm', None, 'gx', 'gy'), may hold values from -0.3 to 0.3
- obs_cells: int32 [8, 4, 2, 1024], P('tm', 'gx', 'gy'), may hold values from 0 to 65535
- step_count: int32 [8], P('tm'), may hold values from 1 to 4, as said below
Outputs:
- lagrange_next: float32 [8, 8, 256, 256], P('tm', None, 'gx', 'gy')
- obs_lagrange_next: float32 [8, 4, 2, 1024], P('tm', 'gx', 'gy')
- increment_next: float32 [8, 8, 256, 256], P('tm', None, 'gx', 'gy')
- residual_model: float32 [8, 8, 256, 256], P('tm', None, 'gx', 'gy')
- residual_obs: float32 [8, 4, 2, 1024], P('tm', 'gx', 'gy')
- residual_increment: float32 [8, 8, 256, 256], P('tm', None, 'gx', 'gy')
Inputs may be any that keep to these rules, and one draw needn't show every extreme that they name: `step_count`: each sub-window's number of model steps; at least one sub-window takes 4.
All inputs are finite; a program needn't handle non-finite values.
Results may differ from a plain program's by a relative error of at most 0.0003.
Values sent between devices are 32-bit elements; how exact they have to be, the bound alone decides.
A program may use at most 64 MiB of HBM per device.

v0:
```python
import functools

import jax
import jax.numpy as jnp
from jax import lax
from jax.experimental import pallas as pl
from jax.experimental.pallas import tpu as pltpu
from jax.sharding import PartitionSpec as P

MAXSTEP = 4
DIFFUSION = 0.18
VERTICAL = 0.1
CENTRE = 1.0 - 4.0 * DIFFUSION - 2.0 * VERTICAL
FORWARD, ADJOINT = 0, 1
LOW, HIGH, SIDE = 0, 1, 2
PAD = 8
MESH = pl.DeviceIdType.MESH
F32, BF16 = jnp.float32, jnp.bfloat16


def pieces(value):
    high = value.astype(BF16)
    rest = value - high.astype(F32)
    mid = rest.astype(BF16)
    low = (rest - mid.astype(F32)).astype(BF16)
    return high, mid, low


def kernel(
    sizes,
    lagr_in, obs_lagr_in, incr_in, forcing_in, depart_in, model_var_in, obs_var_in, wind_e_in, wind_n_in,
    cells_in, counts,
    res_m, res_o, res_v, img_m, img_o, img_v, alpha_grid, alpha_line,
    lagr, obs_lagr, incr, forcing, depart, model_var, obs_var, wind_e, wind_n, cells, load_sem,
    field, half_e, half_n, onehot, spread_buf, next_lagr, next_model, next_image, arrived,
    last_image, leaving, row_out, row_in, col_out, col_in, part_out, part_in,
    send_sem, recv_sem, wide_send, wide_recv, part_send, part_recv,
):
    n_tm, n_gx, n_gy = sizes
    subs, levels, rows, lanes = incr.shape
    flat = levels * rows
    end = subs - 1
    inner = pl.ds(PAD, rows)
    before = pl.ds(PAD - 1, rows)
    after = pl.ds(PAD + 1, rows)
    tm, gx, gy = lax.axis_index("tm"), lax.axis_index("gx"), lax.axis_index("gy")
    lane = lax.broadcasted_iota(jnp.int32, (rows, lanes), 1)
    out_edge = jnp.where(gy == 0, lanes - 1, 0)
    sign = jnp.where(gy == 0, -1.0, 1.0)
    at_edge = lane == out_edge
    at_first, at_last = lane == 0, lane == lanes - 1

    loads = [
        pltpu.make_async_copy(src, dst, load_sem.at[at])
        for at, (src, dst) in enumerate((
            (incr_in, incr), (lagr_in, lagr), (wind_e_in, wind_e), (wind_n_in, wind_n),
            (cells_in, cells), (model_var_in, model_var), (forcing_in, forcing),
            (obs_lagr_in, obs_lagr), (obs_var_in, obs_var), (depart_in, depart),
        ))
    ]
    for load in loads:
        load.start()

    row_in[...] = jnp.zeros_like(row_in)
    next_lagr[...] = jnp.zeros_like(next_lagr)
    next_model[...] = jnp.zeros_like(next_model)
    next_image[...] = jnp.zeros_like(next_image)
    arrived[...] = jnp.zeros_like(arrived)
    last_image[...] = jnp.zeros_like(last_image)

    plane = [
        {"gx": lax.rem(gx + a, n_gx), "gy": lax.rem(gy + b, n_gy)}
        for a in range(n_gx) for b in range(n_gy) if a + b > 0
    ]
    column_peers = [{"tm": lax.rem(tm + k, n_tm)} for k in range(1, n_tm)]
    barrier = pltpu.get_barrier_semaphore()
    for peer in plane + column_peers:
        pl.semaphore_signal(barrier, inc=1, device_id=peer, device_id_type=MESH)

    def wide(index, src, dst, step):
        return pltpu.make_async_remote_copy(
            src_ref=src, dst_ref=dst, send_sem=wide_send.at[index], recv_sem=wide_recv.at[index],
            device_id={"tm": lax.rem(tm + step + n_tm, n_tm)}, device_id_type=MESH,
        )

    sent_lagr = wide(0, lagr.at[0], next_lagr, -1)
    sent_model = wide(1, img_m.at[0], next_model, -1)
    sent_forward = wide(2, leaving, arrived, 1)
    sent_image = wide(3, img_m.at[0], next_image, -1)
    sent_last = wide(4, field.at[FORWARD, 0, end, pl.ds(1, levels), inner], last_image, 1)
    not_first, not_last = tm > 0, tm < n_tm - 1

    def sends(kind, turn):
        pairs = []
        for side, axis, to, allowed in (
            (LOW, "gx", lax.rem(gx + n_gx - 1, n_gx), gx > 0),
            (HIGH, "gx", lax.rem(gx + 1, n_gx), gx < n_gx - 1),
            (SIDE, "gy", lax.rem(gy + 1, n_gy), None),
        ):
            if side == SIDE:
                src, dst, back = col_out.at[kind, turn], col_in.at[kind, turn], None
            else:
                src, dst = row_out.at[kind, turn, side], row_in.at[kind, turn, 1 - side]
                back = gx < n_gx - 1 if side == LOW else gx > 0
            arrival = SIDE if side == SIDE else 1 - side
            copy = pltpu.make_async_remote_copy(
                src_ref=src, dst_ref=dst,
                send_sem=send_sem.at[kind, turn, side], recv_sem=recv_sem.at[kind, turn, arrival],
                device_id={axis: to}, device_id_type=MESH,
            )
            pairs.append((copy, allowed, back))
        return pairs

    def guarded(condition, action):
        if condition is None:
            action()
        else:
            pl.when(condition)(action)

    def start_halo(kind, turn):
        for copy, allowed, _ in sends(kind, turn):
            guarded(allowed, copy.start)

    def wait_halo(kind, turn):
        for copy, _, back in sends(kind, turn):
            guarded(back, copy.wait_recv)

    def put(kind, turn, slot, s, level, new, packed):
        field[kind, slot, s, level + 1, inner] = new
        first, last = new[0:1], new[rows - 1 : rows]
        edge = new
        if kind == ADJOINT:
            first = (DIFFUSION + half_e[s, level, PAD : PAD + 1]) * first
            last = (DIFFUSION - half_e[s, level, PAD + rows - 1 : PAD + rows]) * last
            edge = (DIFFUSION + sign * half_n[s, level]) * new
        row_out[kind, turn, LOW, s, level : level + 1] = first
        row_out[kind, turn, HIGH, s, level : level + 1] = last
        at = s * levels + level
        moved = pltpu.roll(edge, lax.rem(at - out_edge + lanes, lanes), 1)
        return jnp.where(lane == at, moved, packed)

    def begin(kind, turn, source):
        packed = jnp.zeros((rows, lanes), F32)
        for s in range(subs):
            for level in range(levels):
                packed = put(kind, turn, 0, s, level, source(s, level), packed)
        col_out[kind, turn] = packed

    def step(kind, operator, j):
        turn = operator * MAXSTEP + j
        slot = lax.rem(j, 2)
        wait_halo(kind, turn)
        following = turn + 1
        packed = jnp.zeros((rows, lanes), F32)
        for s in range(subs):
            running = jnp.broadcast_to(counts[s], (rows, lanes)) > j
            for level in range(levels):
                field[kind, slot, s, level + 1, PAD - 1 : PAD] = (
                    row_in[kind, turn, LOW, s, level : level + 1]
                )
                field[kind, slot, s, level + 1, PAD + rows : PAD + rows + 1] = (
                    row_in[kind, turn, HIGH, s, level : level + 1]
                )
            for level in range(levels):
                at = s * levels + level
                here = field[kind, slot, s, level + 1, inner]
                east = field[kind, slot, s, level + 1, after]
                west = field[kind, slot, s, level + 1, before]
                column = pltpu.roll(col_in[kind, turn], lax.rem(out_edge - at + lanes, lanes), 1)
                column = jnp.where(at_edge, column, 0.0)
                level_sum = field[kind, slot, s, level + 2, inner] + field[kind, slot, s, level, inner]
                wind = half_n[s, level]
                if kind == FORWARD:
                    north = jnp.where(at_last, column, pltpu.roll(here, lanes - 1, 1))
                    south = jnp.where(at_first, column, pltpu.roll(here, 1, 1))
                    stepped = (
                        CENTRE * here
                        + DIFFUSION * ((east + west) + (north + south))
                        + half_e[s, level, inner] * (west - east)
                        + wind * (south - north)
                        + VERTICAL * level_sum
                    )
                else:
                    north = pltpu.roll((DIFFUSION + wind) * here, lanes - 1, 1)
                    south = pltpu.roll((DIFFUSION - wind) * here, 1, 1)
                    stepped = (
                        CENTRE * here
                        + (DIFFUSION - half_e[s, level, before]) * west
                        + (DIFFUSION + half_e[s, level, after]) * east
                        + jnp.where(at_first, column, south)
                        + jnp.where(at_last, column, north)
                        + VERTICAL * level_sum
                    )
                new = jnp.where(running, stepped, here)
                packed = put(kind, following, 1 - slot, s, level, new, packed)

        @pl.when(j < MAXSTEP - 1)
        def _():
            col_out[kind, following] = packed
            start_halo(kind, following)

    def where_lane(s):
        return lax.broadcasted_iota(jnp.int32, (lanes, cells.shape[3]), 0) == lax.rem(cells[s, 0], lanes)

    def observe(s, value):
        turned = value.reshape(flat, lanes).T
        parts = jnp.concatenate(pieces(turned), 0)
        picked = jnp.dot(parts, onehot[s], preferred_element_type=F32)
        whole = (picked[:lanes] + picked[lanes : 2 * lanes]) + picked[2 * lanes :]
        return jnp.sum(jnp.where(where_lane(s), whole, 0.0), 0, keepdims=True)

    def spread(s, value):
        mask = where_lane(s)
        parts = jnp.concatenate(
            [jnp.where(mask, part.astype(F32), 0.0).astype(BF16) for part in pieces(value)], 0
        )
        summed = lax.dot_general(
            onehot[s], parts, (((1,), (1,)), ((), ())), preferred_element_type=F32
        )
        whole = (summed[:, :lanes] + summed[:, lanes : 2 * lanes]) + summed[:, 2 * lanes :]
        return whole.reshape(levels, rows, lanes)

    def sweeps(operator, first_work, second_work):
        def body(pair, carry):
            for half, work in enumerate((first_work, second_work)):
                j = pair * 2 + half
                step(FORWARD, operator, j)
                work(pair)
                step(ADJOINT, operator, j)
            return carry

        lax.fori_loop(0, MAXSTEP // 2, body, 0)

    for kind in (FORWARD, ADJOINT):
        for slot in range(2):
            for s in range(subs):
                for edge in (0, levels + 1):
                    field[kind, slot, s, edge] = jnp.zeros(field.shape[4:], F32)
    loads[0].wait()
    begin(FORWARD, 0, lambda s, level: incr[s, level])
    loads[1].wait()
    pl.semaphore_wait(barrier, len(plane) + len(column_peers))

    @pl.when(not_first)
    def _():
        sent_lagr.start()

    start_halo(FORWARD, 0)
    loads[5].wait()
    loads[6].wait()
    for s in range(subs):
        img_m[s] = forcing[s] - model_var[s] * lagr[s] - incr[s]

    @pl.when(not_first)
    def _():
        sent_model.start()

    loads[2].wait()
    loads[3].wait()
    half_e[...] = jnp.zeros_like(half_e)
    for s in range(subs):
        half_n[s] = 0.5 * wind_n[s]
        half_e[s, :, inner] = 0.5 * wind_e[s]
        half_e[s, :, PAD - 1 : PAD] = jnp.full((levels, 1, lanes), DIFFUSION - 1.0, F32)
        half_e[s, :, PAD + rows : PAD + rows + 1] = jnp.full((levels, 1, lanes), 1.0 - DIFFUSION, F32)
    loads[4].wait()
    for s in range(subs):
        chosen = lax.div(cells[s, 0], lanes)
        place = lax.broadcasted_iota(jnp.int32, (flat, cells.shape[3]), 0)
        onehot[s] = jnp.where(place == chosen, 1.0, 0.0).astype(BF16)
    for load in loads[7:]:
        load.wait()

    @pl.when(not_last)
    def _():
        sent_lagr.wait_recv()

    begin(ADJOINT, 0, lambda s, level: lagr[s + 1, level] if s < end else next_lagr[level])
    start_halo(ADJOINT, 0)

    def first_spread(s):
        spread_buf[s] = spread(s, obs_lagr[s, 0])

    def first_observe(s):
        res_o[s, 0] = depart[s, 0] - (obs_var[s, 0] * obs_lagr[s, 0] + observe(s, incr[s]))

    sweeps(0, first_spread, first_observe)
    leaving[...] = field[FORWARD, 0, end, pl.ds(1, levels), inner]

    @pl.when(not_last)
    def _():
        sent_forward.start()
        sent_model.wait_recv()

    @pl.when(not_first)
    def _():
        sent_model.wait_send()

    live = jnp.where(not_last, 1.0, 0.0)
    for s in range(subs):
        res_v[s] = field[ADJOINT, 0, s, pl.ds(1, levels), inner] - lagr[s] - spread_buf[s]
    res_m[0] = img_m[0]
    for s in range(1, subs):
        res_m[s] = img_m[s] + field[FORWARD, 0, s - 1, pl.ds(1, levels), inner]
    next_model[...] = live * (next_model[...] + field[FORWARD, 0, end, pl.ds(1, levels), inner])

    begin(FORWARD, MAXSTEP, lambda s, level: res_v[s, level])
    start_halo(FORWARD, MAXSTEP)
    begin(ADJOINT, MAXSTEP, lambda s, level: res_m[s + 1, level] if s < end else next_model[level])
    start_halo(ADJOINT, MAXSTEP)

    def second_spread(s):
        spread_buf[s] = spread(s, res_o[s, 0])

    def second_observe(s):
        img_o[s, 0] = obs_var[s, 0] * res_o[s, 0] + observe(s, res_v[s])

    @pl.when(not_first)
    def _():
        sent_forward.wait_recv()

    res_m[0] = res_m[0] + arrived[...]
    for s in range(subs):
        img_m[s] = model_var[s] * res_m[s] + res_v[s]

    @pl.when(not_first)
    def _():
        sent_image.start()

    sweeps(1, second_spread, second_observe)

    @pl.when(not_last)
    def _():
        sent_last.start()
        sent_image.wait_recv()

    cross = jnp.zeros((rows, lanes), F32)
    square = jnp.zeros((rows, lanes), F32)
    for s in range(subs):
        for level in range(levels):
            image = res_m[s, level] - field[ADJOINT, 0, s, level + 1, inner] + spread_buf[s, level]
            img_v[s, level] = image
            cross = cross + res_v[s, level] * image
            square = square + image * image
    for s in range(1, subs):
        for level in range(levels):
            image = img_m[s, level] - field[FORWARD, 0, s - 1, level + 1, inner]
            img_m[s, level] = image
            cross = cross + res_m[s, level] * image
            square = square + image * image
    alone = jnp.where(not_first, 0.0, 1.0)
    for level in range(levels):
        image = live * (next_image[level] - field[FORWARD, 0, end, level + 1, inner])
        cross = cross + next_model[level] * image
        square = square + image * image
        image = alone * img_m[0, level]
        cross = cross + res_m[0, level] * image
        square = square + image * image
    obs_cross = jnp.zeros((1, cells.shape[3]), F32)
    obs_square = jnp.zeros((1, cells.shape[3]), F32)
    for s in range(subs):
        obs_cross = obs_cross + res_o[s, 0] * img_o[s, 0]
        obs_square = obs_square + img_o[s, 0] * img_o[s, 0]

    def folded(grid, line):
        tile = jnp.sum(grid.reshape(rows // 8, 8, lanes), 0)
        for at in range(0, line.shape[1], lanes):
            piece = line[:, at : at + lanes]
            head = lax.broadcasted_iota(jnp.int32, (8, lanes), 0) == 0
            tile = tile + jnp.where(head, jnp.broadcast_to(piece, (8, lanes)), 0.0)
        return tile

    both = jnp.concatenate([folded(cross, obs_cross), folded(square, obs_square)], 0)
    base = 0
    for phase, targets in enumerate((plane, column_peers)):
        part_out[phase] = both
        copies = []
        for target in targets:
            copy = pltpu.make_async_remote_copy(
                src_ref=part_out.at[phase], dst_ref=part_in.at[base],
                send_sem=part_send.at[base], recv_sem=part_recv.at[base],
                device_id=target, device_id_type=MESH,
            )
            copy.start()
            copies.append((copy, base))
            base += 1
        for copy, slot in copies:
            copy.wait_recv()
            both = both + part_in[slot]
        for copy, _ in copies:
            copy.wait_send()
    total_cross = jnp.sum(jnp.sum(both[:8], 0, keepdims=True), 1, keepdims=True)
    total_square = jnp.sum(jnp.sum(both[8:], 0, keepdims=True), 1, keepdims=True)
    alpha = total_cross / (total_square + 1e-06)
    alpha_grid[0, 0] = jnp.broadcast_to(alpha, alpha_grid.shape[2:])
    alpha_line[0, 0] = jnp.broadcast_to(alpha, alpha_line.shape[2:])

    @pl.when(not_first)
    def _():
        sent_last.wait_recv()
        sent_lagr.wait_send()
        sent_image.wait_send()

    img_m[0] = img_m[0] - last_image[...]

    @pl.when(not_last)
    def _():
        sent_forward.wait_send()
        sent_last.wait_send()

    def drain(turn, carry):
        for kind in (FORWARD, ADJOINT):
            for copy, allowed, _ in sends(kind, turn):
                guarded(allowed, copy.wait_send)
        return carry

    lax.fori_loop(0, 2 * MAXSTEP, drain, 0)


def shards(sizes, *operands):
    lagrange, obs_lagrange, increment = operands[:3]
    subs, levels, rows, lanes = increment.shape
    nobs = obs_lagrange.shape[3]
    n_tm, n_gx, n_gy = sizes
    grid = jax.ShapeDtypeStruct(increment.shape, F32)
    line = jax.ShapeDtypeStruct(obs_lagrange.shape, F32)
    state = pltpu.VMEM((levels, rows, lanes), F32)
    turns = 2 * MAXSTEP
    partners = n_gx * n_gy - 1 + n_tm - 1
    vmem = pl.BlockSpec(memory_space=pltpu.VMEM)
    hbm = pl.BlockSpec(memory_space=pltpu.HBM)
    res_m, res_o, res_v, img_m, img_o, img_v, alpha, alpha_line = pl.pallas_call(
        functools.partial(kernel, sizes),
        out_shape=(grid, line, grid, grid, line, grid, jax.ShapeDtypeStruct((1, 1, 1, lanes), F32),
                   jax.ShapeDtypeStruct((1, 1, 1, nobs), F32)),
        in_specs=[hbm] * 10 + [pl.BlockSpec(memory_space=pltpu.SMEM)],
        out_specs=[vmem] * 8,
        scratch_shapes=[
            *(pltpu.VMEM(operand.shape, operand.dtype) for operand in operands[:10]),
            pltpu.SemaphoreType.DMA((10,)),
            pltpu.VMEM((2, 2, subs, levels + 2, rows + 2 * PAD, lanes), F32),
            pltpu.VMEM((subs, levels, rows + 2 * PAD, lanes), F32),
            pltpu.VMEM((subs, levels, rows, lanes), F32),
            pltpu.VMEM((subs, levels * rows, nobs), BF16),
            pltpu.VMEM((subs, levels, rows, lanes), F32),
            state, state, state, state, state, state,
            pltpu.VMEM((2, turns + 1, 2, subs, levels, lanes), F32),
            pltpu.VMEM((2, turns, 2, subs, levels, lanes), F32),
            pltpu.VMEM((2, turns, rows, lanes), F32),
            pltpu.VMEM((2, turns, rows, lanes), F32),
            pltpu.VMEM((2, 16, lanes), F32),
            pltpu.VMEM((partners, 16, lanes), F32),
            pltpu.SemaphoreType.DMA((2, turns, 3)),
            pltpu.SemaphoreType.DMA((2, turns, 3)),
            pltpu.SemaphoreType.DMA((5,)),
            pltpu.SemaphoreType.DMA((5,)),
            pltpu.SemaphoreType.DMA((partners,)),
            pltpu.SemaphoreType.DMA((partners,)),
        ],
        compiler_params=pltpu.CompilerParams(
            collective_id=0, has_side_effects=True, vmem_limit_bytes=60 * 1024 * 1024
        ),
    )(*operands)
    return (
        lagrange + alpha * res_m,
        obs_lagrange + alpha_line * res_o,
        increment + alpha * res_v,
        res_m - alpha * img_m,
        res_o - alpha_line * img_o,
        res_v - alpha * img_v,
    )


def solution(mesh):
    sizes = (mesh.shape["tm"], mesh.shape["gx"], mesh.shape["gy"])
    state, line = P("tm", None, "gx", "gy"), P("tm", "gx", "gy", None)
    return jax.shard_map(
        functools.partial(shards, sizes),
        mesh=mesh,
        in_specs=(state, line, state, state, line, state, line, state, state, line, P("tm")),
        out_specs=(state, line, state, state, line, state),
        check_vma=False,
    )
```

profile of v0, /device:TPU:0, one launch (start us, length us, event | category | flops | bytes accessed | tf_op | source)
XLA Modules:
  0.0 71.8 jit_solution(15911374319752343103)
XLA Ops:
  0.6 0.0 copy-start.1
  0.6 0.0 copy-start
  0.7 66.2 %shard_map.154 = (f32[2,8,64,128]{3,2,1,0:T(8,128)}, f32[2,1,1,1024]{3,2,1,0:T(1,128)}, f32[2,8,64,128]{3,2,1,0:T(8,128)}, f32[2,8,64,128]{3,2,1,0:T(8,128)}, f3...) custom-call(f32[2,8,64,128]{3,2,1,0:T(8,128)} %lagr_in.1, ...), custom_call_target="tpu_custom_call" | custom-call | tf_op jit(solution)/shard_map/pallas_call | solution.py:432
  66.8 0.0 copy-start.6
  66.9 0.0 copy-done.1
  66.9 0.0 copy-done
  66.9 0.5 copy-done.6
  67.4 0.0 copy-start.2
  67.4 0.0 copy-start.3
  67.4 0.0 copy-start.4
  67.4 3.1 %multiply_subtract_fusion = (f32[2,8,64,128]{3,2,1,0:T(8,128)}, f32[2,8,64,128]{3,2,1,0:T(8,128)}, f32[2,8,64,128]{3,2,1,0:T(8,128)}, f32[2,8,64,128]{3,2,1,0:T(8,128)}) fusion(f32[2,8,64,128]{3,2,1,0:T(8,128)} %get-tuple-element.18, f32[2,8,64,128]{3,2,1,0:T(8,128)} %get-tuple-element.21, f32[128]{0:T(128)S(1)} %bitcast.3, f32[2,8,64,128]{3,2,1,0:T(8,128)S(1)} %copy-done.1, ...), kind=kLoop, calls=%fused_computation | loop fusion | flops 1048576 | bytes 5243392 | tf_op jit(solution)/shard_map/sub | solution.py:470
  70.5 0.0 copy-start.5
  70.5 0.0 copy-done.2
  70.5 0.0 copy-done.3
  70.6 0.0 copy-done.4
  70.6 0.6 copy-done.5
  71.2 0.6 multiply_subtract_fusion.2
Async XLA Ops:
  0.6 66.2 %copy-start.1 = (f32[2,8,64,128]{3,2,1,0:T(8,128)S(1)}, f32[2,8,64,128]{3,2,1,0:T(8,128)}, u32[]{:S(2)}) copy-start(f32[2,8,64,128]{3,2,1,0:T(8,128)} %incr_in.1) | copy-start | bytes 1572868
  0.6 66.2 %copy-start = (f32[2,8,64,128]{3,2,1,0:T(8,128)S(1)}, f32[2,8,64,128]{3,2,1,0:T(8,128)}, u32[]{:S(2)}) copy-start(f32[2,8,64,128]{3,2,1,0:T(8,128)} %lagr_in.1) | copy-start | bytes 1572868
  66.8 0.6 copy-start.6
  67.4 3.1 %copy-start.2 = (f32[2,1,1,1024]{3,2,1,0:T(1,128)S(1)}, f32[2,1,1,1024]{3,2,1,0:T(1,128)}, u32[]{:S(2)}) copy-start(f32[2,1,1,1024]{3,2,1,0:T(1,128)} %obs_lagr_in.1) | copy-start | bytes 24580
  67.4 3.1 %copy-start.3 = (f32[2,1,1,1024]{3,2,1,0:T(1,128)S(1)}, f32[2,1,1,1024]{3,2,1,0:T(1,128)}, u32[]{:S(2)}) copy-start(f32[2,1,1,1024]{3,2,1,0:T(1,128)} %get-tuple-element.17) | copy-start | bytes 24580
  67.4 3.1 %copy-start.4 = (f32[2,1,1,1024]{3,2,1,0:T(1,128)S(1)}, f32[2,1,1,1024]{3,2,1,0:T(1,128)}, u32[]{:S(2)}) copy-start(f32[2,1,1,1024]{3,2,1,0:T(1,128)} %get-tuple-element.20) | copy-start | bytes 24580
  70.5 0.7 copy-start.5
where the time goes:
time: 72 us; the launch traced here: 71.8 us
  Pallas kernels  66.2 us (92%)
  other arithmetic  3.73 us (5%)
  local copies, waits for them, and re-layouts  1.22 us (2%)
    pallas_call x1, Pallas kernels, shards(): pl.pallas_call(functools.partial(kernel, sizes), out_shape=(grid, line, g...  66.2 us
    sub x1, other arithmetic, shards(): res_v - alpha * img_v  3.11 us

commit v1 on v0

--- a/solution.py
+++ b/solution.py
@@ -32,7 +32,7 @@
     cells_in, counts,
     res_m, res_o, res_v, img_m, img_o, img_v, alpha_grid, alpha_line,
     lagr, obs_lagr, incr, forcing, depart, model_var, obs_var, wind_e, wind_n, cells, load_sem,
-    field, half_e, half_n, onehot, spread_buf, next_lagr, next_model, next_image, arrived,
+    field_00, field_01, field_10, field_11, half_e, half_n, onehot, spread_buf, next_lagr, next_model, next_image, arrived,
     last_image, leaving, row_out, row_in, col_out, col_in, part_out, part_in,
     send_sem, recv_sem, wide_send, wide_recv, part_send, part_recv,
 ):
@@ -40,6 +40,7 @@
     subs, levels, rows, lanes = incr.shape
     flat = levels * rows
     end = subs - 1
+    field = ((field_00, field_01), (field_10, field_11))
     inner = pl.ds(PAD, rows)
     before = pl.ds(PAD - 1, rows)
     after = pl.ds(PAD + 1, rows)
@@ -87,7 +88,7 @@
     sent_model = wide(1, img_m.at[0], next_model, -1)
     sent_forward = wide(2, leaving, arrived, 1)
     sent_image = wide(3, img_m.at[0], next_image, -1)
-    sent_last = wide(4, field.at[FORWARD, 0, end, pl.ds(1, levels), inner], last_image, 1)
+    sent_last = wide(4, field_00.at[end, pl.ds(1, levels), inner], last_image, 1)
     not_first, not_last = tm > 0, tm < n_tm - 1
 
     def sends(kind, turn):
@@ -126,7 +127,7 @@
             guarded(back, copy.wait_recv)
 
     def put(kind, turn, slot, s, level, new, packed):
-        field[kind, slot, s, level + 1, inner] = new
+        field[kind][slot][s, level + 1, inner] = new
         first, last = new[0:1], new[rows - 1 : rows]
         edge = new
         if kind == ADJOINT:
@@ -146,29 +147,28 @@
                 packed = put(kind, turn, 0, s, level, source(s, level), packed)
         col_out[kind, turn] = packed
 
-    def step(kind, operator, j):
+    def step(kind, operator, j, slot):
         turn = operator * MAXSTEP + j
-        slot = lax.rem(j, 2)
         wait_halo(kind, turn)
         following = turn + 1
         packed = jnp.zeros((rows, lanes), F32)
         for s in range(subs):
             running = jnp.broadcast_to(counts[s], (rows, lanes)) > j
             for level in range(levels):
-                field[kind, slot, s, level + 1, PAD - 1 : PAD] = (
+                field[kind][slot][s, level + 1, PAD - 1 : PAD] = (
                     row_in[kind, turn, LOW, s, level : level + 1]
                 )
-                field[kind, slot, s, level + 1, PAD + rows : PAD + rows + 1] = (
+                field[kind][slot][s, level + 1, PAD + rows : PAD + rows + 1] = (
                     row_in[kind, turn, HIGH, s, level : level + 1]
                 )
             for level in range(levels):
                 at = s * levels + level
-                here = field[kind, slot, s, level + 1, inner]
-                east = field[kind, slot, s, level + 1, after]
-                west = field[kind, slot, s, level + 1, before]
+                here = field[kind][slot][s, level + 1, inner]
+                east = field[kind][slot][s, level + 1, after]
+                west = field[kind][slot][s, level + 1, before]
                 column = pltpu.roll(col_in[kind, turn], lax.rem(out_edge - at + lanes, lanes), 1)
                 column = jnp.where(at_edge, column, 0.0)
-                level_sum = field[kind, slot, s, level + 2, inner] + field[kind, slot, s, level, inner]
+                level_sum = field[kind][slot][s, level + 2, inner] + field[kind][slot][s, level, inner]
                 wind = half_n[s, level]
                 if kind == FORWARD:
                     north = jnp.where(at_last, column, pltpu.roll(here, lanes - 1, 1))
@@ -224,9 +224,9 @@
         def body(pair, carry):
             for half, work in enumerate((first_work, second_work)):
                 j = pair * 2 + half
-                step(FORWARD, operator, j)
+                step(FORWARD, operator, j, half)
                 work(pair)
-                step(ADJOINT, operator, j)
+                step(ADJOINT, operator, j, half)
             return carry
 
         lax.fori_loop(0, MAXSTEP // 2, body, 0)
@@ -235,7 +235,7 @@
         for slot in range(2):
             for s in range(subs):
                 for edge in (0, levels + 1):
-                    field[kind, slot, s, edge] = jnp.zeros(field.shape[4:], F32)
+                    field[kind][slot][s, edge] = jnp.zeros(field_00.shape[2:], F32)
     loads[0].wait()
     begin(FORWARD, 0, lambda s, level: incr[s, level])
     loads[1].wait()
@@ -285,7 +285,7 @@
         res_o[s, 0] = depart[s, 0] - (obs_var[s, 0] * obs_lagr[s, 0] + observe(s, incr[s]))
 
     sweeps(0, first_spread, first_observe)
-    leaving[...] = field[FORWARD, 0, end, pl.ds(1, levels), inner]
+    leaving[...] = field[FORWARD][0][end, pl.ds(1, levels), inner]
 
     @pl.when(not_last)
     def _():
@@ -298,11 +298,11 @@
 
     live = jnp.where(not_last, 1.0, 0.0)
     for s in range(subs):
-        res_v[s] = field[ADJOINT, 0, s, pl.ds(1, levels), inner] - lagr[s] - spread_buf[s]
+        res_v[s] = field[ADJOINT][0][s, pl.ds(1, levels), inner] - lagr[s] - spread_buf[s]
     res_m[0] = img_m[0]
     for s in range(1, subs):
-        res_m[s] = img_m[s] + field[FORWARD, 0, s - 1, pl.ds(1, levels), inner]
-    next_model[...] = live * (next_model[...] + field[FORWARD, 0, end, pl.ds(1, levels), inner])
+        res_m[s] = img_m[s] + field[FORWARD][0][s - 1, pl.ds(1, levels), inner]
+    next_model[...] = live * (next_model[...] + field[FORWARD][0][end, pl.ds(1, levels), inner])
 
     begin(FORWARD, MAXSTEP, lambda s, level: res_v[s, level])
     start_halo(FORWARD, MAXSTEP)
@@ -338,19 +338,19 @@
     square = jnp.zeros((rows, lanes), F32)
     for s in range(subs):
         for level in range(levels):
-            image = res_m[s, level] - field[ADJOINT, 0, s, level + 1, inner] + spread_buf[s, level]
+            image = res_m[s, level] - field[ADJOINT][0][s, level + 1, inner] + spread_buf[s, level]
             img_v[s, level] = image
             cross = cross + res_v[s, level] * image
             square = square + image * image
     for s in range(1, subs):
         for level in range(levels):
-            image = img_m[s, level] - field[FORWARD, 0, s - 1, level + 1, inner]
+            image = img_m[s, level] - field[FORWARD][0][s - 1, level + 1, inner]
             img_m[s, level] = image
             cross = cross + res_m[s, level] * image
             square = square + image * image
     alone = jnp.where(not_first, 0.0, 1.0)
     for level in range(levels):
-        image = live * (next_image[level] - field[FORWARD, 0, end, level + 1, inner])
+        image = live * (next_image[level] - field[FORWARD][0][end, level + 1, inner])
         cross = cross + next_model[level] * image
         square = square + image * image
         image = alone * img_m[0, level]
@@ -417,6 +417,51 @@
     lax.fori_loop(0, 2 * MAXSTEP, drain, 0)
 
 
+def update(*refs):
+    sources, targets, held, made = refs[:11], refs[11:17], refs[17:28], refs[28:34]
+    load_sem, small_sem, store_sem = refs[34:]
+    subs = held[0].shape[0]
+    small = [pltpu.make_async_copy(sources[6 + at], held[6 + at], small_sem.at[at]) for at in range(5)]
+    loads = [
+        [pltpu.make_async_copy(sources[at].at[s], held[at].at[s], load_sem.at[at, s]) for at in range(6)]
+        for s in range(subs)
+    ]
+    stores = [
+        [pltpu.make_async_copy(made[at].at[s], targets[at].at[s], store_sem.at[at, s]) for at in range(6)]
+        for s in range(subs)
+    ]
+    small[3].start()
+    for group in loads:
+        for load in group:
+            load.start()
+    for at in (0, 1, 2, 4):
+        small[at].start()
+    lagr, incr, res_m, res_v, img_m, img_v, obs_lagr, res_o, img_o, alpha_grid, alpha_line = held
+    small[3].wait()
+    alpha = alpha_grid[0]
+    for s in range(subs):
+        for load in loads[s]:
+            load.wait()
+        made[0][s] = lagr[s] + alpha * res_m[s]
+        stores[s][0].start()
+        made[2][s] = incr[s] + alpha * res_v[s]
+        stores[s][2].start()
+        made[3][s] = res_m[s] - alpha * img_m[s]
+        stores[s][3].start()
+        made[5][s] = res_v[s] - alpha * img_v[s]
+        stores[s][5].start()
+    for at in (0, 1, 2, 4):
+        small[at].wait()
+    for s in range(subs):
+        made[1][s] = obs_lagr[s] + alpha_line[0] * res_o[s]
+        stores[s][1].start()
+        made[4][s] = res_o[s] - alpha_line[0] * img_o[s]
+        stores[s][4].start()
+    for group in stores:
+        for store in group:
+            store.wait()
+
+
 def shards(sizes, *operands):
     lagrange, obs_lagrange, increment = operands[:3]
     subs, levels, rows, lanes = increment.shape
@@ -438,7 +483,7 @@
         scratch_shapes=[
             *(pltpu.VMEM(operand.shape, operand.dtype) for operand in operands[:10]),
             pltpu.SemaphoreType.DMA((10,)),
-            pltpu.VMEM((2, 2, subs, levels + 2, rows + 2 * PAD, lanes), F32),
+            *[pltpu.VMEM((subs, levels + 2, rows + 2 * PAD, lanes), F32)] * 4,
             pltpu.VMEM((subs, levels, rows + 2 * PAD, lanes), F32),
             pltpu.VMEM((subs, levels, rows, lanes), F32),
             pltpu.VMEM((subs, levels * rows, nobs), BF16),
@@ -461,14 +506,21 @@
             collective_id=0, has_side_effects=True, vmem_limit_bytes=60 * 1024 * 1024
         ),
     )(*operands)
-    return (
-        lagrange + alpha * res_m,
-        obs_lagrange + alpha_line * res_o,
-        increment + alpha * res_v,
-        res_m - alpha * img_m,
-        res_o - alpha_line * img_o,
-        res_v - alpha * img_v,
-    )
+    sources = (lagrange, increment, res_m, res_v, img_m, img_v, obs_lagrange, res_o, img_o, alpha, alpha_line)
+    return pl.pallas_call(
+        update,
+        out_shape=(grid, line, grid, grid, line, grid),
+        in_specs=[hbm] * len(sources),
+        out_specs=[hbm] * 6,
+        scratch_shapes=[
+            *(pltpu.VMEM(source.shape, source.dtype) for source in sources),
+            *(pltpu.VMEM(shape.shape, F32) for shape in (grid, line, grid, grid, line, grid)),
+            pltpu.SemaphoreType.DMA((6, subs)),
+            pltpu.SemaphoreType.DMA((5,)),
+            pltpu.SemaphoreType.DMA((6, subs)),
+        ],
+        compiler_params=pltpu.CompilerParams(vmem_limit_bytes=60 * 1024 * 1024),
+    )(*sources)
 
 
 def solution(mesh):

time: 72 us -> 69.7 us (0.968)
  other arithmetic: 3.73 us -> 0 us
  Pallas kernels: 66.2 us -> 68.9 us
  local copies, waits for them, and re-layouts: 1.22 us -> 0 us
    sub x2 -> x0, other arithmetic: 3.73 us -> none  [the longest x1 3.11 us: shards(): res_v - alpha * img_v]
    pallas_call x0 -> x1, Pallas kernels: none -> 3.09 us  [shards(): pl.pallas_call(update, out_shape=(grid, line, grid, grid, line, grid), in...]
    unnamed x14 -> x0, local copies, waits for them, and re-layouts: 1.22 us -> none
where the time goes in v1:
time: 69.7 us; the launch traced here: 69.5 us
  Pallas kernels  68.9 us (99%)
    pallas_call x1, Pallas kernels, shards(): pl.pallas_call(functools.partial(kernel, sizes), out_shape=(grid, line, g...  65.8 us
    pallas_call x1, Pallas kernels, shards(): pl.pallas_call(update, out_shape=(grid, line, grid, grid, line, grid), in...  3.09 us

profile of v1, /device:TPU:0, one launch (start us, length us, event | category | flops | bytes accessed | tf_op | source)
XLA Modules:
  0.0 69.5 jit_solution(4751819590264307392)
XLA Ops:
  0.6 65.8 %shard_map.154 = (f32[2,8,64,128]{3,2,1,0:T(8,128)}, f32[2,1,1,1024]{3,2,1,0:T(1,128)}, f32[2,8,64,128]{3,2,1,0:T(8,128)}, f32[2,8,64,128]{3,2,1,0:T(8,128)}, f3...) custom-call(f32[2,8,64,128]{3,2,1,0:T(8,128)} %refs_0_.1, ...), custom_call_target="tpu_custom_call" | custom-call | tf_op jit(solution)/shard_map/pallas_call | solution.py:477
  66.5 3.1 %shard_map.155 = (f32[2,8,64,128]{3,2,1,0:T(8,128)}, f32[2,1,1,1024]{3,2,1,0:T(1,128)}, f32[2,8,64,128]{3,2,1,0:T(8,128)}, f32[2,8,64,128]{3,2,1,0:T(8,128)}, f3...) custom-call(f32[2,8,64,128]{3,2,1,0:T(8,128)} %refs_0_.1, f32[2,8,64,128]{3,2,1,0:T(8,128)} %refs_1_.1, ...), custom_call_target="tpu_custom_call" | custom-call | tf_op jit(solution)/shard_map/pallas_call | solution.py:510

commit v2 on v1

--- a/solution.py
+++ b/solution.py
@@ -32,7 +32,7 @@
     cells_in, counts,
     res_m, res_o, res_v, img_m, img_o, img_v, alpha_grid, alpha_line,
     lagr, obs_lagr, incr, forcing, depart, model_var, obs_var, wind_e, wind_n, cells, load_sem,
-    field_00, field_01, field_10, field_11, half_e, half_n, onehot, spread_buf, next_lagr, next_model, next_image, arrived,
+    field_00, field_01, field_10, field_11, half_e, half_n, from_west, from_east, later, onehot, spread_buf, next_lagr, next_model, next_image, arrived,
     last_image, leaving, row_out, row_in, col_out, col_in, part_out, part_in,
     send_sem, recv_sem, wide_send, wide_recv, part_send, part_recv,
 ):
@@ -134,65 +134,73 @@
             first = (DIFFUSION + half_e[s, level, PAD : PAD + 1]) * first
             last = (DIFFUSION - half_e[s, level, PAD + rows - 1 : PAD + rows]) * last
             edge = (DIFFUSION + sign * half_n[s, level]) * new
-        row_out[kind, turn, LOW, s, level : level + 1] = first
-        row_out[kind, turn, HIGH, s, level : level + 1] = last
+        row_out[kind, turn, LOW, s, pl.ds(level, 1)] = first
+        row_out[kind, turn, HIGH, s, pl.ds(level, 1)] = last
         at = s * levels + level
         moved = pltpu.roll(edge, lax.rem(at - out_edge + lanes, lanes), 1)
         return jnp.where(lane == at, moved, packed)
 
+    def over_levels(visit):
+        group = 4
+        turns_of = levels // group
+
+        def body(at, packed):
+            s, first = lax.div(at, turns_of), lax.rem(at, turns_of) * group
+            for k in range(group):
+                packed = visit(s, first + k, packed)
+            return packed
+
+        return lax.fori_loop(0, subs * turns_of, body, jnp.zeros((rows, lanes), F32))
+
     def begin(kind, turn, source):
-        packed = jnp.zeros((rows, lanes), F32)
-        for s in range(subs):
-            for level in range(levels):
-                packed = put(kind, turn, 0, s, level, source(s, level), packed)
-        col_out[kind, turn] = packed
+        def visit(s, level, packed):
+            return put(kind, turn, 0, s, level, source[s, level], packed)
+
+        col_out[kind, turn] = over_levels(visit)
 
     def step(kind, operator, j, slot):
         turn = operator * MAXSTEP + j
         wait_halo(kind, turn)
         following = turn + 1
-        packed = jnp.zeros((rows, lanes), F32)
-        for s in range(subs):
+        source = field[kind][slot]
+
+        def visit(s, level, packed):
+            source[s, level + 1, PAD - 1 : PAD] = row_in[kind, turn, LOW, s, pl.ds(level, 1)]
+            source[s, level + 1, PAD + rows : PAD + rows + 1] = row_in[kind, turn, HIGH, s, pl.ds(level, 1)]
             running = jnp.broadcast_to(counts[s], (rows, lanes)) > j
-            for level in range(levels):
-                field[kind][slot][s, level + 1, PAD - 1 : PAD] = (
-                    row_in[kind, turn, LOW, s, level : level + 1]
+            at = s * levels + level
+            here = source[s, level + 1, inner]
+            east = source[s, level + 1, after]
+            west = source[s, level + 1, before]
+            column = pltpu.roll(col_in[kind, turn], lax.rem(out_edge - at + lanes, lanes), 1)
+            column = jnp.where(at_edge, column, 0.0)
+            level_sum = source[s, level + 2, inner] + source[s, level, inner]
+            wind = half_n[s, level]
+            if kind == FORWARD:
+                north = jnp.where(at_last, column, pltpu.roll(here, lanes - 1, 1))
+                south = jnp.where(at_first, column, pltpu.roll(here, 1, 1))
+                stepped = (
+                    CENTRE * here
+                    + DIFFUSION * ((east + west) + (north + south))
+                    + half_e[s, level, inner] * (west - east)
+                    + wind * (south - north)
+                    + VERTICAL * level_sum
                 )
-                field[kind][slot][s, level + 1, PAD + rows : PAD + rows + 1] = (
-                    row_in[kind, turn, HIGH, s, level : level + 1]
+            else:
+                north = pltpu.roll((DIFFUSION + wind) * here, lanes - 1, 1)
+                south = pltpu.roll((DIFFUSION - wind) * here, 1, 1)
+                stepped = (
+                    CENTRE * here
+                    + from_west[s, level] * west
+                    + from_east[s, level] * east
+                    + jnp.where(at_first, column, south)
+                    + jnp.where(at_last, column, north)
+                    + VERTICAL * level_sum
                 )
-            for level in range(levels):
-                at = s * levels + level
-                here = field[kind][slot][s, level + 1, inner]
-                east = field[kind][slot][s, level + 1, after]
-                west = field[kind][slot][s, level + 1, before]
-                column = pltpu.roll(col_in[kind, turn], lax.rem(out_edge - at + lanes, lanes), 1)
-                column = jnp.where(at_edge, column, 0.0)
-                level_sum = field[kind][slot][s, level + 2, inner] + field[kind][slot][s, level, inner]
-                wind = half_n[s, level]
-                if kind == FORWARD:
-                    north = jnp.where(at_last, column, pltpu.roll(here, lanes - 1, 1))
-                    south = jnp.where(at_first, column, pltpu.roll(here, 1, 1))
-                    stepped = (
-                        CENTRE * here
-                        + DIFFUSION * ((east + west) + (north + south))
-                        + half_e[s, level, inner] * (west - east)
-                        + wind * (south - north)
-                        + VERTICAL * level_sum
-                    )
-                else:
-                    north = pltpu.roll((DIFFUSION + wind) * here, lanes - 1, 1)
-                    south = pltpu.roll((DIFFUSION - wind) * here, 1, 1)
-                    stepped = (
-                        CENTRE * here
-                        + (DIFFUSION - half_e[s, level, before]) * west
-                        + (DIFFUSION + half_e[s, level, after]) * east
-                        + jnp.where(at_first, column, south)
-                        + jnp.where(at_last, column, north)
-                        + VERTICAL * level_sum
-                    )
-                new = jnp.where(running, stepped, here)
-                packed = put(kind, following, 1 - slot, s, level, new, packed)
+            new = jnp.where(running, stepped, here)
+            return put(kind, following, 1 - slot, s, level, new, packed)
+
+        packed = over_levels(visit)
 
         @pl.when(j < MAXSTEP - 1)
         def _():
@@ -237,7 +245,7 @@
                 for edge in (0, levels + 1):
                     field[kind][slot][s, edge] = jnp.zeros(field_00.shape[2:], F32)
     loads[0].wait()
-    begin(FORWARD, 0, lambda s, level: incr[s, level])
+    begin(FORWARD, 0, incr)
     loads[1].wait()
     pl.semaphore_wait(barrier, len(plane) + len(column_peers))
 
@@ -263,6 +271,9 @@
         half_e[s, :, inner] = 0.5 * wind_e[s]
         half_e[s, :, PAD - 1 : PAD] = jnp.full((levels, 1, lanes), DIFFUSION - 1.0, F32)
         half_e[s, :, PAD + rows : PAD + rows + 1] = jnp.full((levels, 1, lanes), 1.0 - DIFFUSION, F32)
+    for s in range(subs):
+        from_west[s] = DIFFUSION - half_e[s, :, before]
+        from_east[s] = DIFFUSION + half_e[s, :, after]
     loads[4].wait()
     for s in range(subs):
         chosen = lax.div(cells[s, 0], lanes)
@@ -275,7 +286,10 @@
     def _():
         sent_lagr.wait_recv()
 
-    begin(ADJOINT, 0, lambda s, level: lagr[s + 1, level] if s < end else next_lagr[level])
+    for s in range(end):
+        later[s] = lagr[s + 1]
+    later[end] = next_lagr[...]
+    begin(ADJOINT, 0, later)
     start_halo(ADJOINT, 0)
 
     def first_spread(s):
@@ -304,9 +318,12 @@
         res_m[s] = img_m[s] + field[FORWARD][0][s - 1, pl.ds(1, levels), inner]
     next_model[...] = live * (next_model[...] + field[FORWARD][0][end, pl.ds(1, levels), inner])
 
-    begin(FORWARD, MAXSTEP, lambda s, level: res_v[s, level])
+    begin(FORWARD, MAXSTEP, res_v)
     start_halo(FORWARD, MAXSTEP)
-    begin(ADJOINT, MAXSTEP, lambda s, level: res_m[s + 1, level] if s < end else next_model[level])
+    for s in range(end):
+        later[s] = res_m[s + 1]
+    later[end] = next_model[...]
+    begin(ADJOINT, MAXSTEP, later)
     start_halo(ADJOINT, MAXSTEP)
 
     def second_spread(s):
@@ -485,7 +502,7 @@
             pltpu.SemaphoreType.DMA((10,)),
             *[pltpu.VMEM((subs, levels + 2, rows + 2 * PAD, lanes), F32)] * 4,
             pltpu.VMEM((subs, levels, rows + 2 * PAD, lanes), F32),
-            pltpu.VMEM((subs, levels, rows, lanes), F32),
+            *[pltpu.VMEM((subs, levels, rows, lanes), F32)] * 4,
             pltpu.VMEM((subs, levels * rows, nobs), BF16),
             pltpu.VMEM((subs, levels, rows, lanes), F32),
             state, state, state, state, state, state,

time: 69.7 us -> 66.8 us (0.958)
  Pallas kernels: 68.9 us -> 66 us
    pallas_call x1, Pallas kernels: 65.8 us -> 62.9 us  [shards(): pl.pallas_call(functools.partial(kernel, sizes), out_shape=(grid, line, g...]
where the time goes in v2:
time: 66.8 us; the launch traced here: 66.6 us
  Pallas kernels  66 us (99%)
    pallas_call x1, Pallas kernels, shards(): pl.pallas_call(functools.partial(kernel, sizes), out_shape=(grid, line, g...  62.9 us
    pallas_call x1, Pallas kernels, shards(): pl.pallas_call(update, out_shape=(grid, line, grid, grid, line, grid), in...  3.09 us

profile of v2, /device:TPU:0, one launch (start us, length us, event | category | flops | bytes accessed | tf_op | source)
XLA Modules:
  0.0 66.6 jit_solution(15714712488193314357)
XLA Ops:
  0.6 62.9 %shard_map.154 = (f32[2,8,64,128]{3,2,1,0:T(8,128)}, f32[2,1,1,1024]{3,2,1,0:T(1,128)}, f32[2,8,64,128]{3,2,1,0:T(8,128)}, f32[2,8,64,128]{3,2,1,0:T(8,128)}, f3...) custom-call(f32[2,8,64,128]{3,2,1,0:T(8,128)} %refs_0_.1, ...), custom_call_target="tpu_custom_call" | custom-call | tf_op jit(solution)/shard_map/pallas_call | solution.py:494
  63.5 3.1 %shard_map.155 = (f32[2,8,64,128]{3,2,1,0:T(8,128)}, f32[2,1,1,1024]{3,2,1,0:T(1,128)}, f32[2,8,64,128]{3,2,1,0:T(8,128)}, f32[2,8,64,128]{3,2,1,0:T(8,128)}, f3...) custom-call(f32[2,8,64,128]{3,2,1,0:T(8,128)} %refs_0_.1, f32[2,8,64,128]{3,2,1,0:T(8,128)} %refs_1_.1, ...), custom_call_target="tpu_custom_call" | custom-call | tf_op jit(solution)/shard_map/pallas_call | solution.py:527

commit v3 on v2

--- a/solution.py
+++ b/solution.py
@@ -88,7 +88,7 @@
     sent_model = wide(1, img_m.at[0], next_model, -1)
     sent_forward = wide(2, leaving, arrived, 1)
     sent_image = wide(3, img_m.at[0], next_image, -1)
-    sent_last = wide(4, field_00.at[end, pl.ds(1, levels), inner], last_image, 1)
+    sent_last = wide(4, field_10.at[end, pl.ds(1, levels), inner], last_image, 1)
     not_first, not_last = tm > 0, tm < n_tm - 1
 
     def sends(kind, turn):
@@ -126,8 +126,8 @@
         for copy, _, back in sends(kind, turn):
             guarded(back, copy.wait_recv)
 
-    def put(kind, turn, slot, s, level, new, packed):
-        field[kind][slot][s, level + 1, inner] = new
+    def put(kind, turn, target, s, level, new, packed):
+        target[s, level + 1, inner] = new
         first, last = new[0:1], new[rows - 1 : rows]
         edge = new
         if kind == ADJOINT:
@@ -154,15 +154,15 @@
 
     def begin(kind, turn, source):
         def visit(s, level, packed):
-            return put(kind, turn, 0, s, level, source[s, level], packed)
+            return put(kind, turn, field[kind ^ (turn // MAXSTEP)][0], s, level, source[s, level], packed)
 
         col_out[kind, turn] = over_levels(visit)
 
-    def step(kind, operator, j, slot):
+    def step(kind, operator, j):
         turn = operator * MAXSTEP + j
         wait_halo(kind, turn)
-        following = turn + 1
-        source = field[kind][slot]
+        following = turn + 1 if j < MAXSTEP - 1 else 2 * MAXSTEP
+        source, target = (field[kind ^ operator][(j + at) % 2] for at in range(2))
 
         def visit(s, level, packed):
             source[s, level + 1, PAD - 1 : PAD] = row_in[kind, turn, LOW, s, pl.ds(level, 1)]
@@ -198,12 +198,11 @@
                     + VERTICAL * level_sum
                 )
             new = jnp.where(running, stepped, here)
-            return put(kind, following, 1 - slot, s, level, new, packed)
+            return put(kind, following, target, s, level, new, packed)
 
         packed = over_levels(visit)
 
-        @pl.when(j < MAXSTEP - 1)
-        def _():
+        if j < MAXSTEP - 1:
             col_out[kind, following] = packed
             start_halo(kind, following)
 
@@ -228,17 +227,6 @@
         whole = (summed[:, :lanes] + summed[:, lanes : 2 * lanes]) + summed[:, 2 * lanes :]
         return whole.reshape(levels, rows, lanes)
 
-    def sweeps(operator, first_work, second_work):
-        def body(pair, carry):
-            for half, work in enumerate((first_work, second_work)):
-                j = pair * 2 + half
-                step(FORWARD, operator, j, half)
-                work(pair)
-                step(ADJOINT, operator, j, half)
-            return carry
-
-        lax.fori_loop(0, MAXSTEP // 2, body, 0)
-
     for kind in (FORWARD, ADJOINT):
         for slot in range(2):
             for s in range(subs):
@@ -259,10 +247,6 @@
     for s in range(subs):
         img_m[s] = forcing[s] - model_var[s] * lagr[s] - incr[s]
 
-    @pl.when(not_first)
-    def _():
-        sent_model.start()
-
     loads[2].wait()
     loads[3].wait()
     half_e[...] = jnp.zeros_like(half_e)
@@ -282,6 +266,20 @@
     for load in loads[7:]:
         load.wait()
 
+    def first_spread(s):
+        spread_buf[s] = spread(s, obs_lagr[s, 0])
+
+    def first_observe(s):
+        res_o[s, 0] = depart[s, 0] - (obs_var[s, 0] * obs_lagr[s, 0] + observe(s, incr[s]))
+
+    def second_spread(s):
+        spread_buf[s] = spread(s, res_o[s, 0])
+
+    def second_observe(s):
+        img_o[s, 0] = obs_var[s, 0] * res_o[s, 0] + observe(s, res_v[s])
+
+    step(FORWARD, 0, 0)
+
     @pl.when(not_last)
     def _():
         sent_lagr.wait_recv()
@@ -292,51 +290,60 @@
     begin(ADJOINT, 0, later)
     start_halo(ADJOINT, 0)
 
-    def first_spread(s):
-        spread_buf[s] = spread(s, obs_lagr[s, 0])
-
-    def first_observe(s):
-        res_o[s, 0] = depart[s, 0] - (obs_var[s, 0] * obs_lagr[s, 0] + observe(s, incr[s]))
-
-    sweeps(0, first_spread, first_observe)
-    leaving[...] = field[FORWARD][0][end, pl.ds(1, levels), inner]
+    @pl.when(not_first)
+    def _():
+        sent_model.start()
+
+    for s in range(end):
+        first_spread(s)
+    step(FORWARD, 0, 1)
+    first_spread(end)
+    step(ADJOINT, 0, 0)
+    for s in range(end):
+        first_observe(s)
+    step(FORWARD, 0, 2)
+    first_observe(end)
+    step(ADJOINT, 0, 1)
+    step(FORWARD, 0, 3)
+    forward = field[FORWARD][0]
+    leaving[...] = forward[end, pl.ds(1, levels), inner]
 
     @pl.when(not_last)
     def _():
         sent_forward.start()
+
+    step(ADJOINT, 0, 2)
+
+    @pl.when(not_last)
+    def _():
         sent_model.wait_recv()
 
-    @pl.when(not_first)
-    def _():
-        sent_model.wait_send()
-
     live = jnp.where(not_last, 1.0, 0.0)
-    for s in range(subs):
-        res_v[s] = field[ADJOINT][0][s, pl.ds(1, levels), inner] - lagr[s] - spread_buf[s]
-    res_m[0] = img_m[0]
     for s in range(1, subs):
-        res_m[s] = img_m[s] + field[FORWARD][0][s - 1, pl.ds(1, levels), inner]
-    next_model[...] = live * (next_model[...] + field[FORWARD][0][end, pl.ds(1, levels), inner])
-
-    begin(FORWARD, MAXSTEP, res_v)
-    start_halo(FORWARD, MAXSTEP)
+        res_m[s] = img_m[s] + forward[s - 1, pl.ds(1, levels), inner]
+    next_model[...] = live * (next_model[...] + leaving[...])
     for s in range(end):
         later[s] = res_m[s + 1]
     later[end] = next_model[...]
     begin(ADJOINT, MAXSTEP, later)
     start_halo(ADJOINT, MAXSTEP)
-
-    def second_spread(s):
-        spread_buf[s] = spread(s, res_o[s, 0])
-
-    def second_observe(s):
-        img_o[s, 0] = obs_var[s, 0] * res_o[s, 0] + observe(s, res_v[s])
+    step(ADJOINT, 0, 3)
+    for s in range(subs):
+        res_v[s] = field[ADJOINT][0][s, pl.ds(1, levels), inner] - lagr[s] - spread_buf[s]
+    begin(FORWARD, MAXSTEP, res_v)
+    start_halo(FORWARD, MAXSTEP)
+    step(ADJOINT, 1, 0)
+    for s in range(end):
+        second_spread(s)
+    step(FORWARD, 1, 0)
+    second_spread(end)
 
     @pl.when(not_first)
     def _():
+        sent_model.wait_send()
         sent_forward.wait_recv()
 
-    res_m[0] = res_m[0] + arrived[...]
+    res_m[0] = img_m[0] + arrived[...]
     for s in range(subs):
         img_m[s] = model_var[s] * res_m[s] + res_v[s]
 
@@ -344,7 +351,15 @@
     def _():
         sent_image.start()
 
-    sweeps(1, second_spread, second_observe)
+    step(ADJOINT, 1, 1)
+    for s in range(end):
+        second_observe(s)
+    step(FORWARD, 1, 1)
+    second_observe(end)
+    step(ADJOINT, 1, 2)
+    step(FORWARD, 1, 2)
+    step(ADJOINT, 1, 3)
+    step(FORWARD, 1, 3)
 
     @pl.when(not_last)
     def _():
@@ -355,19 +370,19 @@
     square = jnp.zeros((rows, lanes), F32)
     for s in range(subs):
         for level in range(levels):
-            image = res_m[s, level] - field[ADJOINT][0][s, level + 1, inner] + spread_buf[s, level]
+            image = res_m[s, level] - field[FORWARD][0][s, level + 1, inner] + spread_buf[s, level]
             img_v[s, level] = image
             cross = cross + res_v[s, level] * image
             square = square + image * image
     for s in range(1, subs):
         for level in range(levels):
-            image = img_m[s, level] - field[FORWARD][0][s - 1, level + 1, inner]
+            image = img_m[s, level] - field[ADJOINT][0][s - 1, level + 1, inner]
             img_m[s, level] = image
             cross = cross + res_m[s, level] * image
             square = square + image * image
     alone = jnp.where(not_first, 0.0, 1.0)
     for level in range(levels):
-        image = live * (next_image[level] - field[FORWARD][0][end, level + 1, inner])
+        image = live * (next_image[level] - field[ADJOINT][0][end, level + 1, inner])
         cross = cross + next_model[level] * image
         square = square + image * image
         image = alone * img_m[0, level]

time: 66.8 us -> 60.2 us (0.901)
  Pallas kernels: 66 us -> 59.4 us
    pallas_call x1, Pallas kernels: 62.9 us -> 56.3 us  [shards(): pl.pallas_call(functools.partial(kernel, sizes), out_shape=(grid, line, g...]
where the time goes in v3:
time: 60.2 us; the launch traced here: 60 us
  Pallas kernels  59.4 us (99%)
  between operations  0.64 us (1%)
    pallas_call x1, Pallas kernels, shards(): pl.pallas_call(functools.partial(kernel, sizes), out_shape=(grid, line, g...  56.3 us
    pallas_call x1, Pallas kernels, shards(): pl.pallas_call(update, out_shape=(grid, line, grid, grid, line, grid), in...  3.09 us

profile of v3, /device:TPU:0, one launch (start us, length us, event | category | flops | bytes accessed | tf_op | source)
XLA Modules:
  0.0 60.0 jit_solution(1629117326653580929)
XLA Ops:
  0.6 56.3 %shard_map.154 = (f32[2,8,64,128]{3,2,1,0:T(8,128)}, f32[2,1,1,1024]{3,2,1,0:T(1,128)}, f32[2,8,64,128]{3,2,1,0:T(8,128)}, f32[2,8,64,128]{3,2,1,0:T(8,128)}, f3...) custom-call(f32[2,8,64,128]{3,2,1,0:T(8,128)} %refs_0_.1, ...), custom_call_target="tpu_custom_call" | custom-call | tf_op jit(solution)/shard_map/pallas_call | solution.py:509
  56.9 3.1 %shard_map.155 = (f32[2,8,64,128]{3,2,1,0:T(8,128)}, f32[2,1,1,1024]{3,2,1,0:T(1,128)}, f32[2,8,64,128]{3,2,1,0:T(8,128)}, f32[2,8,64,128]{3,2,1,0:T(8,128)}, f3...) custom-call(f32[2,8,64,128]{3,2,1,0:T(8,128)} %refs_0_.1, f32[2,8,64,128]{3,2,1,0:T(8,128)} %refs_1_.1, ...), custom_call_target="tpu_custom_call" | custom-call | tf_op jit(solution)/shard_map/pallas_call | solution.py:542
